TPU v7x, 32 devices: a whole 2x2x4 slice. The times are simulated.
32 devices in a mesh: row: 8 (over y, x, core), col: 4 (over z).
Axes of the slice: x: 2, y: 2, z: 4, core: 2. Of those that a mesh axis runs over, the one named last changes fastest.
Arguments:
- values: bfloat16 [192, 24, 64, 64], P(('row', 'col')), may hold values from -6 to 6
- columns: int32 [192, 24], replicated, may hold values from 0 to 191, as said below
Outputs:
- purified: bfloat16 [192, 24, 64, 64], P(('row', 'col'))
Inputs may be any that keep to these rules, and one draw needn't show every extreme that they name: Each block row i has 24 distinct block columns, each (i + o) modulo 192 with -12 <= o <= 12, in increasing order of o; the offsets -12 and 12 are always among them.
All inputs are finite; a program needn't handle non-finite values.
Results may differ from a plain program's by a relative error of at most 0.012.
Values may be sent and summed in bfloat16 or wider, within the bound.
A program may use at most 128 MiB of HBM per device.

v0:
```python
import math

import jax
import jax.numpy as jnp
import numpy as np
from jax import lax
from jax.sharding import PartitionSpec as P

REACH = 12


def passed_along(block, axis, distance):
    devices = range(lax.axis_size(axis))
    route = [((i - distance) % len(devices), i) for i in devices]
    return lax.ppermute(block, axis, route)


def within_reach(field):
    received = {}
    for direction in (1, -1):
        if direction == 1:
            outgoing = field
        else:
            outgoing = field
        received[direction] = passed_along(outgoing, ("row", "col"), direction)
    far_parts = {}
    for direction in (1, -1):
        if direction == 1:
            outgoing = field
        else:
            outgoing = field
        far_parts[direction] = passed_along(outgoing, ("row", "col"), 2 * direction)
    pieces = [far_parts[1], received[1], field, received[-1], far_parts[-1]]
    return jnp.concatenate(pieces, axis=0)


def band_product(left_band, extended, scale):
    rows = left_band.shape[0]
    width = left_band.shape[1]
    block = left_band.shape[2]
    reach = (width - 1) // 2
    stride = width + 1
    padded = jnp.pad(extended, ((0, 0), (0, 1), (0, 0), (0, 0)))
    slot_grid = np.arange(width)[:, None]
    out_grid = np.arange(width)[None, :]
    valid_table = np.abs(out_grid - slot_grid) <= reach
    halves = [(0, reach + 1), (reach + 1, width)]

    def one_row(args):
        left_row, row_id = args
        total = jnp.zeros((width, block, block), jnp.float32)
        for first, last in halves:
            count = last - first
            window = lax.dynamic_slice_in_dim(padded, row_id + first, count, 0)
            flat = window.reshape(count * stride, block, block)
            flat = jnp.pad(flat, ((2 * reach, 2 * reach), (0, 0), (0, 0)))
            begin = 3 * reach - first
            skewed = flat[begin : begin + count * width].reshape(count, width, block, block)
            valid = jnp.asarray(valid_table[first:last])
            skewed = jnp.where(valid[:, :, None, None], skewed, jnp.zeros((), skewed.dtype))
            total = total + jnp.einsum(
                "axy,awyz->wxz", left_row[first:last], skewed, preferred_element_type=jnp.float32
            )
        return total

    row_ids = jnp.arange(rows, dtype=jnp.int32)
    return scale * lax.map(one_row, (left_band, row_ids))


def shards(values, columns):
    rows = values.shape[0]
    knz = values.shape[1]
    block = values.shape[2]
    total_rows = columns.shape[0]
    width = 2 * REACH + 1
    scale = 0.6 / math.sqrt(knz * block)
    start = lax.axis_index(("row", "col")) * rows
    mine = lax.dynamic_slice_in_dim(columns, start, rows, 0)
    row_ids = start + jnp.arange(rows, dtype=jnp.int32)
    offset_index = (mine - row_ids[:, None] + REACH) % total_rows
    band_ids = jnp.arange(width, dtype=jnp.int32)
    onehot_bool = offset_index[:, :, None] == band_ids[None, None, :]
    onehot = onehot_bool.astype(jnp.bfloat16)
    keep = jnp.any(onehot_bool, axis=1).astype(jnp.float32)[:, :, None, None]
    band = jnp.einsum("isw,isxy->iwxy", onehot, values, preferred_element_type=jnp.float32).astype(
        jnp.bfloat16
    )
    extended = within_reach(band)
    square = (band_product(band, extended, scale) * keep).astype(jnp.bfloat16)
    cube = band_product(square, extended, scale) * keep
    band = (3.0 * square.astype(jnp.float32) - 2.0 * cube).astype(jnp.bfloat16)
    purified = jnp.einsum("isw,iwxy->isxy", onehot, band, preferred_element_type=jnp.float32)
    return purified.astype(jnp.bfloat16)


def solution(mesh):
    placed = (P(("row", "col"), None, None, None), P())
    return jax.shard_map(
        shards,
        mesh=mesh,
        in_specs=placed,
        out_specs=P(("row", "col"), None, None, None),
        check_vma=False,
    )
```

profile of v0, /device:TPU:27, one launch (start us, length us, event | category | flops | bytes accessed | tf_op | source)
XLA Modules:
  0.0 666.9 jit_solution(10226506128608417446)
XLA Ops:
  11.9 106.0 %collective-permute-done = bf16[6,25,64,64]{3,2,1,0:T(8,128)(2,1)} collective-permute-done((bf16[6,25,64,64]{3,2,1,0:T(8,128)(2,1)}, bf16[6,25,64,64]{3,2,1,0:T(8,128)(2,1)}, u32[]{:S(2)}, u32[]{:S(2)}) %collective-permute-start) | collective-permute-done | bytes 1228832 | tf_op jit(solution)/shard_map/ppermute | solution.py:15
  121.3 47.4 %collective-permute-done.1 = bf16[6,25,64,64]{3,2,1,0:T(8,128)(2,1)} collective-permute-done((bf16[6,25,64,64]{3,2,1,0:T(8,128)(2,1)}, bf16[6,25,64,64]{3,2,1,0:T(8,128)(2,1)}, u32[]{:S(2)}, u32[]{:S(2)}) %collective-permute-start.1) | collective-permute-done | bytes 1228832 | tf_op jit(solution)/shard_map/ppermute | solution.py:15
  176.6 151.7 %collective-permute-done.3 = bf16[6,25,64,64]{3,2,1,0:T(8,128)(2,1)} collective-permute-done((bf16[6,25,64,64]{3,2,1,0:T(8,128)(2,1)}, bf16[6,25,64,64]{3,2,1,0:T(8,128)(2,1)}, u32[]{:S(2)}, u32[]{:S(2)}) %collective-permute-start.3) | collective-permute-done | bytes 1228832 | tf_op jit(solution)/shard_map/ppermute | solution.py:15
  331.8 5.7 copy.57
  337.6 6.8 %pad.21.clone = bf16[30,26,64,64]{3,2,1,0:T(8,128)(2,1)} pad(bf16[30,25,64,64]{3,2,1,0:T(8,128)(2,1)S(1)} %copy.57, bf16[]{:T(256)} %constant.118.clone.1), padding=0_0x0_1x0_0x0_0 | pad | bytes 12533762 | tf_op jit(solution)/shard_map/jit(_pad)/pad | solution.py:43
  347.3 147.9 %while.26 = (s32[]{:T(128)}, f32[6,25,64,64]{2,3,1,0:T(8,128)}, s32[6]{0:T(128)S(1)}, bf16[30,26,64,64]{3,2,1,0:T(8,128)(2,1)}, bf16[6,25,64,64]{3,2,1,0:T(8,128...) while((s32[]{:T(128)}, f32[6,25,64,64]{2,3,1,0:T(8,128)}, ...), condition=%wide.region_1.2_spmd.clone, body=%wide.region_0.1_spmd.sunk.clone.sunk | while | flops 330342400 | bytes 30615904 | solution.py:67
  349.1 4.8 constant_dynamic-slice_fusion.8
  357.5 3.9 convolution_bitcast_fusion.6
  363.2 3.9 constant_dynamic-slice_fusion.9
  373.8 4.8 constant_dynamic-slice_fusion.8
  382.1 3.9 convolution_bitcast_fusion.6
  387.9 3.9 constant_dynamic-slice_fusion.9
  398.4 4.8 constant_dynamic-slice_fusion.8
  406.8 3.9 convolution_bitcast_fusion.6
  412.5 3.9 constant_dynamic-slice_fusion.9
  423.1 4.8 constant_dynamic-slice_fusion.8
  431.4 3.9 convolution_bitcast_fusion.6
  437.1 3.9 constant_dynamic-slice_fusion.9
  447.7 4.8 constant_dynamic-slice_fusion.8
  456.1 3.9 convolution_bitcast_fusion.6
  461.8 3.9 constant_dynamic-slice_fusion.9
  472.4 4.8 constant_dynamic-slice_fusion.8
  480.7 3.9 convolution_bitcast_fusion.6
  486.4 3.9 constant_dynamic-slice_fusion.9
  495.1 4.4 multiply_convert_fusion
  502.3 148.0 %while.27 = (s32[]{:T(128)}, f32[6,25,64,64]{2,3,1,0:T(8,128)}, s32[6]{0:T(128)S(1)}, bf16[30,26,64,64]{3,2,1,0:T(8,128)(2,1)}, bf16[6,25,64,64]{2,3,1,0:T(8,128...) while((s32[]{:T(128)}, f32[6,25,64,64]{2,3,1,0:T(8,128)}, ...), condition=%wide.region_4.5_spmd.clone, body=%wide.region_3.4_spmd.sunk.clone.sunk | while | flops 330342400 | bytes 30615904 | solution.py:67
  504.2 4.8 constant_dynamic-slice_fusion.10
  508.9 3.6 fusion.42
  512.5 3.8 convolution_bitcast_fusion.7
  518.3 3.9 constant_dynamic-slice_fusion.11
  528.9 4.8 constant_dynamic-slice_fusion.10
  537.2 3.9 convolution_bitcast_fusion.7
  543.0 3.9 constant_dynamic-slice_fusion.11
  553.5 4.8 constant_dynamic-slice_fusion.10
  561.9 3.8 convolution_bitcast_fusion.7
  567.6 3.9 constant_dynamic-slice_fusion.11
  578.2 4.8 constant_dynamic-slice_fusion.10
  586.6 3.9 convolution_bitcast_fusion.7
  592.3 3.9 constant_dynamic-slice_fusion.11
  602.9 4.8 constant_dynamic-slice_fusion.10
  611.2 3.9 convolution_bitcast_fusion.7
  617.0 3.9 constant_dynamic-slice_fusion.11
  627.5 4.8 constant_dynamic-slice_fusion.10
  632.3 3.6 fusion.42
  635.9 3.9 convolution_bitcast_fusion.7
  641.6 3.9 constant_dynamic-slice_fusion.11
  650.3 6.4 subtract_convert_fusion
  656.7 5.4 copy.45
  (85 shorter events, 137.9 us)
Async XLA Ops:
  0.0 1.7 copy-start
  1.7 10.1 %copy-start.4 = (s32[6,24]{1,0:T(8,128)}, s32[6,24]{1,0:T(8,128)S(1)}, u32[]{:S(2)}) copy-start(s32[6,24]{1,0:T(8,128)S(1)} %copy.31) | copy-start | bytes 1732
  3.7 1.6 copy-start.2
  7.7 110.1 %collective-permute-start = (bf16[6,25,64,64]{3,2,1,0:T(8,128)(2,1)}, bf16[6,25,64,64]{3,2,1,0:T(8,128)(2,1)}, u32[]{:S(2)}, u32[]{:S(2)}) collective-permute-start(bf16[6,25,64,64]{3,2,1,0:T(8,128)(2,1)} %copy.33), channel_id=1, source_target_pairs={{30,0},{31,1},{0,2},{1,3},{2,4},{3,5},{4,6},{5,7},{6,8},{7,9},{8,1... | collective-permute-start | bytes 3686408 | tf_op jit(solution)/shard_map/ppermute | solution.py:15
  9.3 159.3 %collective-permute-start.1 = (bf16[6,25,64,64]{3,2,1,0:T(8,128)(2,1)}, bf16[6,25,64,64]{3,2,1,0:T(8,128)(2,1)}, u32[]{:S(2)}, u32[]{:S(2)}) collective-permute-start(bf16[6,25,64,64]{3,2,1,0:T(8,128)(2,1)} %copy.33), channel_id=1, source_target_pairs={{31,0},{0,1},{1,2},{2,3},{3,4},{4,5},{5,6},{6,7},{7,8},{8,9},{9,10... | collective-permute-start | bytes 3686408 | tf_op jit(solution)/shard_map/ppermute | solution.py:15
  11.8 161.2 %collective-permute-start.2 = (bf16[6,25,64,64]{3,2,1,0:T(8,128)(2,1)}, bf16[6,25,64,64]{3,2,1,0:T(8,128)(2,1)}, u32[]{:S(2)}, u32[]{:S(2)}) collective-permute-start(bf16[6,25,64,64]{3,2,1,0:T(8,128)(2,1)} %copy.33), channel_id=1, source_target_pairs={{1,0},{2,1},{3,2},{4,3},{5,4},{6,5},{7,6},{8,7},{9,8},{10,9},{11,1... | collective-permute-start | bytes 3686408 | tf_op jit(solution)/shard_map/ppermute | solution.py:15
  11.8 316.5 %collective-permute-start.3 = (bf16[6,25,64,64]{3,2,1,0:T(8,128)(2,1)}, bf16[6,25,64,64]{3,2,1,0:T(8,128)(2,1)}, u32[]{:S(2)}, u32[]{:S(2)}) collective-permute-start(bf16[6,25,64,64]{3,2,1,0:T(8,128)(2,1)} %copy.33), channel_id=1, source_target_pairs={{2,0},{3,1},{4,2},{5,3},{6,4},{7,5},{8,6},{9,7},{10,8},{11,9},{12,... | collective-permute-start | bytes 3686408 | tf_op jit(solution)/shard_map/ppermute | solution.py:15
  11.9 160.3 %copy-start.3 = (bf16[6,25,64,64]{3,1,2,0:T(8,128)(2,1)S(1)}, bf16[6,25,64,64]{3,1,2,0:T(8,128)(2,1)}, u32[]{:S(2)}) copy-start(bf16[6,25,64,64]{3,1,2,0:T(8,128)(2,1)} %copy-done.2) | copy-start | bytes 3686404
  344.4 2.9 copy-start.6
  344.4 2.9 copy-start.7
  656.7 5.4 copy-start.5
  656.7 10.1 %copy-start.1 = (bf16[6,24,64,64]{3,2,1,0:T(8,128)(2,1)S(1)}, bf16[6,24,64,64]{3,2,1,0:T(8,128)(2,1)}, u32[]{:S(2)}) copy-start(bf16[6,24,64,64]{3,2,1,0:T(8,128)(2,1)} %param.10) | copy-start | bytes 3538948
where the time goes:
time: 670 us; the launch traced here: 667 us
  waiting for transfers between devices  305 us (46%)
  local copies, waits for them, and re-layouts  157 us (23%)
  matrix products  93 us (14%)
  other arithmetic  70.3 us (10%)
  loops' own time  37.8 us (6%)
    ppermute x4, waiting for transfers between devices, passed_along(): return lax.ppermute(block, axis, route)  305 us
    dynamic_slice x24, local copies, waits for them, and re-layouts, one_row(): window = lax.dynamic_slice_in_dim(padded, row_id + first, count, 0)  104 us
    dot_general x24, matrix products, one_row(): jnp.einsum('axy,awyz->wxz', left_row[first:last], skewed, preferred_eleme...  88.3 us
    select_n x24, other arithmetic, one_row(): jnp.where(valid[:, :, None, None], skewed, jnp.zeros((), skewed.dtype))  58.4 us
    another operation x2, loops' own time, band_product(): return scale * lax.map(one_row, (left_band, row_ids))  37.8 us
    unnamed x21, local copies, waits for them, and re-layouts  19.3 us
  transfers between devices with their start and end apart: 4, of which 3 were waited for; matrix products, arithmetic and copies ran while one was open for 2% of the time, Pallas kernels for 0%

commit v1 on v0

v1 whole, which is shorter than its diff:
```python
import functools
import math

import jax
import jax.numpy as jnp
from jax import lax
from jax.experimental import pallas as pl
from jax.experimental.pallas import tpu as pltpu
from jax.sharding import PartitionSpec as P

REACH = 12
MESH = pl.DeviceIdType.MESH
OWN = -1
NEXT, PREV, NEXT2, PREV2 = 0, 1, 2, 3

NEED = {
    NEXT: lambda c: (0, 12 - c),
    PREV: lambda c: (2 - c, 12),
    NEXT2: lambda c: (0, 9 - c),
    PREV2: lambda c: (5 - c, 12),
}
MIRROR = {NEXT: PREV, PREV: NEXT, NEXT2: PREV2, PREV2: NEXT2, OWN: OWN}


def every(c):
    return (0, 12)


def relay_plan():
    down = {
        3: [(OWN, 0, 2, NEXT, every, 0)],
        2: [(OWN, 0, 1, NEXT, every, 0), (NEXT, 0, 1, NEXT2, every, 0)],
        1: [
            (OWN, 0, 0, NEXT, NEED[NEXT], 0),
            (NEXT, 0, 0, NEXT2, NEED[NEXT2], 0),
            (NEXT, 1, 0, PREV2, lambda c: (9 - c, 12), 0),
            (NEXT2, 1, 0, PREV, NEED[PREV], 0),
            (NEXT2, 1, 1, PREV2, NEED[PREV2], 0),
        ],
        0: [(NEXT2, 1, 0, PREV2, lambda c: (5 - c, 9 - c), 1)],
    }

    def flipped(pairs):
        def f(c):
            first, last = pairs(2 - c)
            return (12 - last, 12 - first)

        return f

    plan = {z: [] for z in range(4)}
    for z in range(4):
        a = down[z]
        b = [
            (MIRROR[s], -dl, 3 - dz, MIRROR[d], flipped(pairs), part)
            for s, dl, dz, d, pairs, part in down[3 - z]
        ]
        both = []
        for i in range(max(len(a), len(b))):
            both += a[i : i + 1] + b[i : i + 1]
        plan[z] = sorted(both, key=lambda t: t[0] != OWN)
    return plan


def kernel(n_rows, n_cols, values_ref, columns_ref, out_ref, pk, rx, rd, sq_ref, fin, send_sem, recv_sem):
    total = columns_ref.shape[0]
    row, col = lax.axis_index("row"), lax.axis_index("col")
    me = row * n_cols + col
    devices = n_rows * n_cols
    relay = n_cols == 4 and n_rows >= 3

    def place(linear):
        return (linear // n_cols, lax.rem(linear, n_cols))

    barrier = pltpu.get_barrier_semaphore()
    if relay:
        greeted = 0
        for dl in (-1, 0, 1):
            for dz in range(4):
                line = lax.rem(row + dl + n_rows, n_rows)
                other = lax.rem(col + dz, 4)
                if dl == 0 and dz == 0:
                    continue
                pl.semaphore_signal(barrier, inc=1, device_id=(line, other), device_id_type=MESH)
                greeted += 1
        pl.semaphore_wait(barrier, greeted)
    else:
        for step in (1, -1, 2, -2):
            other = place(lax.rem(me + step + devices, devices))
            pl.semaphore_signal(barrier, inc=1, device_id=other, device_id_type=MESH)
        pl.semaphore_wait(barrier, 4)

    for r in range(6):
        for p in range(12):
            pk[r, p] = jnp.concatenate([values_ref[r, 2 * p], values_ref[r, 2 * p + 1]], axis=1)

    def chunk(buffer, c, first, last):
        ref = pk if buffer == OWN else rx.at[buffer]
        return ref.at[pl.ds(2 * c, 2), pl.ds(first, last - first)]

    def describe(src, dst, pairs, part, c, sem, device):
        first, last = pairs(c)
        return pltpu.make_async_remote_copy(
            src_ref=chunk(src, c, first, last),
            dst_ref=chunk(dst, c, first, last),
            send_sem=send_sem.at[sem],
            recv_sem=recv_sem.at[dst, part, c],
            device_id=device,
            device_id_type=MESH,
        )

    lane = lax.broadcasted_iota(jnp.int32, (1, 128), 1)
    upper = (lane >= 64).astype(jnp.int32)
    slot = lax.broadcasted_iota(jnp.int32, (1, 24), 1)
    missing = []
    for k in range(30):
        block_row = lax.rem(me * 6 + (k - REACH) + total, total)
        found = columns_ref[pl.ds(block_row, 1), :]
        offset = found - block_row + REACH
        offset = jnp.where(offset < 0, offset + total, offset)
        offset = jnp.where(offset >= total, offset - total, offset)
        same = jnp.where(offset == slot, 1.0, 0.0)
        missing.append(jnp.sum(same, axis=1, keepdims=True).astype(jnp.int32))

    def build(k, read):
        m = missing[k]
        zero = jnp.zeros((64, 128), jnp.bfloat16)
        pair = lambda p: read(p) if 0 <= p < 12 else zero
        shifted = lambda p: jnp.concatenate([pair(p - 1)[:, 64:], pair(p)[:, :64]], axis=1)
        odd = k % 2
        base = (k - REACH + odd) // 2
        for q in range(15):
            p = q - base
            if p < -odd or p > 12 - odd:
                tile = zero
            else:
                w = 2 * p + odd + upper
                before = (w < m).astype(jnp.float32).astype(jnp.bfloat16)
                after = (w > m).astype(jnp.float32).astype(jnp.bfloat16)
                if odd:
                    tile = shifted(p + 1) * before + pair(p) * after
                else:
                    tile = pair(p) * before + shifted(p) * after
            rd[pl.ds(64 * k, 64), pl.ds(128 * q, 128)] = tile

    def run(transfers, incoming, target, meanwhile):
        here = set()
        started = []

        def arrive(dst, part, c, pairs):
            if (dst, part, c) in here:
                return
            here.add((dst, part, c))
            describe(OWN, dst, pairs, part, c, 0, target(0, 0)).wait_recv()

        pairs_of = {(dst, part): pairs for dst, part, pairs in incoming}
        done_own = False
        for src, dl, dz, dst, pairs, part in transfers:
            if src != OWN and not done_own:
                meanwhile()
                done_own = True
            for c in range(3):
                if src != OWN:
                    arrive(src, 0, c, pairs_of[(src, 0)])
                copy = describe(src, dst, pairs, part, c, len(started), target(dl, dz))
                copy.start()
                started.append(copy)
        if not done_own:
            meanwhile()
        for dst, part, pairs in incoming:
            for c in range(3):
                arrive(dst, part, c, pairs)
        return started

    def own_rows():
        for r in range(6):
            build(REACH + r, lambda p, r=r: pk[r, p])

    if relay:
        plan = relay_plan()
        for z in range(4):
            incoming = [
                (t[3], t[5], t[4]) for zz in range(4) for t in plan[zz] if t[2] == z
            ]

            @pl.when(col == z)
            def _(z=z, incoming=incoming):
                target = lambda dl, dz: (
                    lax.rem(row + dl + n_rows, n_rows),
                    jnp.int32(dz),
                )
                started = run(plan[z], incoming, target, lambda: None)
                for copy in started:
                    copy.wait_send()
        own_rows()
    else:
        steps = {NEXT: -1, PREV: 1, NEXT2: -2, PREV2: 2}
        transfers = [(OWN, s, 0, b, NEED[b], 0) for b, s in steps.items()]
        incoming = [(b, 0, NEED[b]) for b in steps]
        target = lambda s, _: place(lax.rem(me + s + devices, devices))
        started = run(transfers, incoming, target, own_rows)
        for copy in started:
            copy.wait_send()

    for buffer, first in ((NEXT, 18), (PREV, 6), (NEXT2, 24), (PREV2, 0)):
        for r in range(6):
            build(first + r, lambda p, b=buffer, r=r: rx[b, r, p])

    scale = 0.6 / math.sqrt(24 * 64)
    spans = [(0, 18), (0, 24), (0, 30), (6, 30), (12, 30)]
    wide = lax.broadcasted_iota(jnp.int32, (1, 384), 1) // 64
    for t, (k0, k1) in enumerate(spans):
        product = jnp.dot(
            rd[768:1152, 64 * k0 : 64 * k1],
            rd[64 * k0 : 64 * k1, 384 * t : 384 * t + 384],
            preferred_element_type=jnp.float32,
        )
        for r in range(6):
            w = wide + (6 * t - r)
            keep = (w >= 0) & (w <= 24) & (w != missing[REACH + r])
            part = product[64 * r : 64 * r + 64] * jnp.where(keep, scale, 0.0)
            sq_ref[64 * r : 64 * r + 64, 384 * t : 384 * t + 384] = part.astype(jnp.bfloat16)
    for t, (k0, k1) in enumerate(spans):
        product = jnp.dot(
            sq_ref[:, 64 * k0 : 64 * k1],
            rd[64 * k0 : 64 * k1, 384 * t : 384 * t + 384],
            preferred_element_type=jnp.float32,
        )
        square = sq_ref[:, 384 * t : 384 * t + 384].astype(jnp.float32)
        fin[:, 384 * t : 384 * t + 384] = 3.0 * square - (2.0 * scale) * product

    for r in range(6):
        m = missing[REACH + r]
        at = lambda c: fin[64 * r : 64 * r + 64, 64 * c : 64 * c + 64]
        for s in range(24):
            before = (s < m).astype(jnp.float32)
            out_ref[r, s] = (at(r + s) * before + at(r + s + 1) * (1.0 - before)).astype(jnp.bfloat16)


def shards(n_rows, n_cols, values, columns):
    return pl.pallas_call(
        functools.partial(kernel, n_rows, n_cols),
        out_shape=jax.ShapeDtypeStruct(values.shape, jnp.bfloat16),
        in_specs=[pl.BlockSpec(memory_space=pltpu.VMEM)] * 2,
        out_specs=pl.BlockSpec(memory_space=pltpu.VMEM),
        scratch_shapes=[
            pltpu.VMEM((6, 12, 64, 128), jnp.bfloat16),
            pltpu.VMEM((4, 6, 12, 64, 128), jnp.bfloat16),
            pltpu.VMEM((1920, 1920), jnp.bfloat16),
            pltpu.VMEM((384, 1920), jnp.bfloat16),
            pltpu.VMEM((384, 1920), jnp.float32),
            pltpu.SemaphoreType.DMA((32,)),
            pltpu.SemaphoreType.DMA((4, 2, 3)),
        ],
        compiler_params=pltpu.CompilerParams(
            collective_id=0, has_side_effects=True, vmem_limit_bytes=48 * 1024 * 1024
        ),
    )(values, columns)


def solution(mesh):
    placed = (P(("row", "col"), None, None, None), P())
    return jax.shard_map(
        functools.partial(shards, mesh.shape["row"], mesh.shape["col"]),
        mesh=mesh,
        in_specs=placed,
        out_specs=P(("row", "col"), None, None, None),
        check_vma=False,
    )
```

time: 670 us -> 92.4 us (0.14)
  waiting for transfers between devices: 305 us -> 0 us
  local copies, waits for them, and re-layouts: 157 us -> 3.9 us
  matrix products: 93 us -> 0 us
  Pallas kernels: 0 us -> 88.3 us
  other arithmetic: 70.3 us -> 0 us
  loops' own time: 37.8 us -> 0 us
    ppermute x4 -> x0, waiting for transfers between devices: 305 us -> none  [passed_along(): return lax.ppermute(block, axis, route)]
    dynamic_slice x36 -> x0, local copies, waits for them, and re-layouts: 111 us -> none  [the longest x24 104 us: one_row(): window = lax.dynamic_slice_in_dim(padded, row_id + first, count, 0)]
    dot_general x26 -> x0, matrix products: 93 us -> none  [the longest x24 88.3 us: one_row(): jnp.einsum('axy,awyz->wxz', left_row[first:last], skewed, preferred_eleme...]
    pallas_call x0 -> x1, Pallas kernels: none -> 88.3 us  [shards(): pl.pallas_call(functools.partial(kernel, n_rows, n_cols), out_shape=jax.S...]
    select_n x25 -> x0, other arithmetic: 59.4 us -> none  [the longest x24 58.4 us: one_row(): jnp.where(valid[:, :, None, None], skewed, jnp.zeros((), skewed.dtype))]
    another operation x2 -> x0, loops' own time: 37.8 us -> none  [band_product(): return scale * lax.map(one_row, (left_band, row_ids))]
    unnamed x21 -> x4, local copies, waits for them, and re-layouts: 19.3 us -> 3.9 us
    convert_element_type x2 -> x0, other arithmetic: 10.8 us -> none  [the longest x1 6.42 us: shards(): band = (3.0 * square.astype(jnp.float32) - 2.0 * cube).astype(jnp.bfloat16)]
  transfers between devices with their start and end apart: 4 -> 0, of which waited for: 3 -> 0; matrix products, arithmetic and copies ran while one was open for 2% -> 0% of each run, Pallas kernels for 0% -> 0%
where the time goes in v1:
time: 92.4 us; the launch traced here: 92.2 us
  Pallas kernels  88.3 us (96%)
  local copies, waits for them, and re-layouts  3.9 us (4%)
    pallas_call x1, Pallas kernels, shards(): pl.pallas_call(functools.partial(kernel, n_rows, n_cols), out_shape=jax.S...  88.3 us
    unnamed x4, local copies, waits for them, and re-layouts  3.9 us

profile of v1, /device:TPU:27, one launch (start us, length us, event | category | flops | bytes accessed | tf_op | source)
XLA Modules:
  0.0 92.2 jit_solution(8180316768547775645)
XLA Ops:
  0.0 0.8 copy.3.columns_ref
  0.8 0.0 copy-start
  0.8 1.7 %copy-done = bf16[6,24,64,64]{3,2,1,0:T(8,128)(2,1)S(1)} copy-done((bf16[6,24,64,64]{3,2,1,0:T(8,128)(2,1)S(1)}, bf16[6,24,64,64]{3,2,1,0:T(8,128)(2,1)}, u32[]{:S(2)}) %copy-start) | copy-done | bytes 1179672
  2.5 88.3 %shard_map.28 = bf16[6,24,64,64]{3,2,1,0:T(8,128)(2,1)S(1)} custom-call(bf16[6,24,64,64]{3,2,1,0:T(8,128)(2,1)S(1)} %copy-done, s32[192,24]{1,0:T(8,128)S(1)} %copy.3.columns_ref), custom_call_target="tpu_custom_call" | custom-call | tf_op jit(solution)/shard_map/pallas_call | solution.py:240
  90.8 1.4 %copy.5 = bf16[6,24,64,64]{3,2,1,0:T(8,128)(2,1)} copy(bf16[6,24,64,64]{3,2,1,0:T(8,128)(2,1)S(1)} %shard_map.28) | data formatting | bytes 2359296
Async XLA Ops:
  0.8 1.7 %copy-start = (bf16[6,24,64,64]{3,2,1,0:T(8,128)(2,1)S(1)}, bf16[6,24,64,64]{3,2,1,0:T(8,128)(2,1)}, u32[]{:S(2)}) copy-start(bf16[6,24,64,64]{3,2,1,0:T(8,128)(2,1)} %values_ref.1) | copy-start | bytes 3538948

commit v2 on v1

v2 whole, which is shorter than its diff:
```python
import functools
import math

import jax
import jax.numpy as jnp
from jax import lax
from jax.experimental import pallas as pl
from jax.experimental.pallas import tpu as pltpu
from jax.sharding import PartitionSpec as P

REACH = 12
MESH = pl.DeviceIdType.MESH
OWN = -1
NEXT, PREV, NEXT2, PREV2 = 0, 1, 2, 3

NEED = {
    NEXT: lambda c: (0, 12 - c),
    PREV: lambda c: (2 - c, 12),
    NEXT2: lambda c: (0, 9 - c),
    PREV2: lambda c: (5 - c, 12),
}
MIRROR = {NEXT: PREV, PREV: NEXT, NEXT2: PREV2, PREV2: NEXT2, OWN: OWN}


def every(c):
    return (0, 12)


def relay_plan():
    down = {
        3: [(OWN, 0, 2, NEXT, every, 0)],
        2: [(OWN, 0, 1, NEXT, every, 0), (NEXT, 0, 1, NEXT2, every, 0)],
        1: [
            (OWN, 0, 0, NEXT, NEED[NEXT], 0),
            (NEXT, 0, 0, NEXT2, NEED[NEXT2], 0),
            (NEXT, 1, 0, PREV2, lambda c: (9 - c, 12), 0),
            (NEXT2, 1, 0, PREV, NEED[PREV], 0),
            (NEXT2, 1, 1, PREV2, NEED[PREV2], 0),
        ],
        0: [(NEXT2, 1, 0, PREV2, lambda c: (5 - c, 9 - c), 1)],
    }

    def flipped(pairs):
        def f(c):
            first, last = pairs(2 - c)
            return (12 - last, 12 - first)

        return f

    plan = {z: [] for z in range(4)}
    for z in range(4):
        a = down[z]
        b = [
            (MIRROR[s], -dl, 3 - dz, MIRROR[d], flipped(pairs), part)
            for s, dl, dz, d, pairs, part in down[3 - z]
        ]
        both = []
        for i in range(max(len(a), len(b))):
            both += a[i : i + 1] + b[i : i + 1]
        plan[z] = sorted(both, key=lambda t: t[0] != OWN)
    return plan


def kernel(
    n_rows, n_cols, values_ref, columns_ref, out_ref, vin, pk, rx, rd, sq_ref, fin, load_sem, send_sem, recv_sem
):
    total = columns_ref.shape[1]
    row, col = lax.axis_index("row"), lax.axis_index("col")
    me = row * n_cols + col
    devices = n_rows * n_cols
    relay = n_cols == 4 and n_rows >= 3

    def place(linear):
        return (linear // n_cols, lax.rem(linear, n_cols))

    loads = [
        pltpu.make_async_copy(
            values_ref.at[pl.ds(2 * c, 2)], vin.at[pl.ds(2 * c, 2)], load_sem.at[c]
        )
        for c in range(3)
    ]
    for load in loads:
        load.start()

    barrier = pltpu.get_barrier_semaphore()
    greeted = 0
    if relay:
        for dl in (-1, 0, 1):
            for dz in range(4):
                line = lax.rem(row + dl + n_rows, n_rows)
                other = lax.rem(col + dz, 4)
                if dl == 0 and dz == 0:
                    continue
                pl.semaphore_signal(barrier, inc=1, device_id=(line, other), device_id_type=MESH)
                greeted += 1
    else:
        for step in (1, -1, 2, -2):
            other = place(lax.rem(me + step + devices, devices))
            pl.semaphore_signal(barrier, inc=1, device_id=other, device_id_type=MESH)
            greeted += 1

    for c in range(3):
        loads[c].wait()
        for r in (2 * c, 2 * c + 1):
            for p in range(12):
                pk[r, p] = jnp.concatenate([vin[r, 2 * p], vin[r, 2 * p + 1]], axis=1)
    pl.semaphore_wait(barrier, greeted)

    def chunk(buffer, c, first, last):
        ref = pk if buffer == OWN else rx.at[buffer]
        return ref.at[pl.ds(2 * c, 2), pl.ds(first, last - first)]

    def describe(src, dst, pairs, part, c, sem, device):
        first, last = pairs(c)
        return pltpu.make_async_remote_copy(
            src_ref=chunk(src, c, first, last),
            dst_ref=chunk(dst, c, first, last),
            send_sem=send_sem.at[sem],
            recv_sem=recv_sem.at[dst, part, c],
            device_id=device,
            device_id_type=MESH,
        )

    class Place:
        def __init__(self, transfers, incoming, target):
            self.transfers, self.incoming, self.target = transfers, incoming, target
            self.here = set()
            self.started = []

        def arrive(self, dst, part, c):
            if (dst, part, c) not in self.here:
                self.here.add((dst, part, c))
                pairs = self.incoming[(dst, part)]
                describe(OWN, dst, pairs, part, c, 0, self.target(0, 0)).wait_recv()

        def arrive_chunk(self, dst, c):
            for d, part in self.incoming:
                if d == dst:
                    self.arrive(dst, part, c)

        def send(self, transfer):
            src, dl, dz, dst, pairs, part = transfer
            for c in range(3):
                if src != OWN:
                    self.arrive(src, 0, c)
                self.started.append((src, dst, pairs, part, c, len(self.started), dl, dz))
                self.copy(*self.started[-1]).start()

        def copy(self, src, dst, pairs, part, c, sem, dl, dz):
            return describe(src, dst, pairs, part, c, sem, self.target(dl, dz))

    if relay:
        plan = relay_plan()
        target = lambda dl, dz: (lax.rem(row + dl + n_rows, n_rows), col * 0 + dz)
        places = [
            Place(
                plan[z],
                {(t[3], t[5]): t[4] for zz in range(4) for t in plan[zz] if t[2] == z},
                target,
            )
            for z in range(4)
        ]
    else:
        steps = {NEXT: -1, PREV: 1, NEXT2: -2, PREV2: 2}
        target = lambda s, _: place(lax.rem(me + s + devices, devices))
        places = [
            Place(
                [(OWN, s, 0, b, NEED[b], 0) for b, s in steps.items()],
                {(b, 0): NEED[b] for b in steps},
                target,
            )
        ]

    def at_each_place(action, which=range(len(places))):
        for z in which:
            if len(places) == 1:
                action(places[z])
            else:

                @pl.when(col == z)
                def _(z=z):
                    action(places[z])

    def send_own(p):
        for t in p.transfers:
            if t[0] == OWN:
                p.send(t)

    at_each_place(send_own)

    lane = lax.broadcasted_iota(jnp.int32, (1, 128), 1)
    upper = (lane >= 64).astype(jnp.int32)
    found = columns_ref[...]
    rows_at = lax.broadcasted_iota(jnp.int32, found.shape, 1)
    offset = found - rows_at + REACH
    offset = jnp.where(offset < 0, offset + total, offset)
    offset = jnp.where(offset >= total, offset - total, offset)
    same = offset == lax.broadcasted_iota(jnp.int32, found.shape, 0)
    counts = jnp.sum(jnp.where(same, 1.0, 0.0), axis=0, keepdims=True)
    row_at = lax.broadcasted_iota(jnp.int32, (1, total), 1)
    missing = []
    for k in range(30):
        block_row = lax.rem(me * 6 + (k - REACH) + total, total)
        one = jnp.where(row_at == block_row, counts, 0.0)
        missing.append(jnp.sum(one, axis=1, keepdims=True).astype(jnp.int32))

    def build(k, read):
        m = missing[k]
        zero = jnp.zeros((64, 128), jnp.bfloat16)
        pair = lambda p: read(p) if 0 <= p < 12 else zero
        shifted = lambda p: jnp.concatenate([pair(p - 1)[:, 64:], pair(p)[:, :64]], axis=1)
        odd = k % 2
        base = (k - REACH + odd) // 2
        for q in range(15):
            p = q - base
            if p < -odd or p > 12 - odd:
                tile = zero
            else:
                w = 2 * p + odd + upper
                before = (w < m).astype(jnp.float32).astype(jnp.bfloat16)
                after = (w > m).astype(jnp.float32).astype(jnp.bfloat16)
                if odd:
                    tile = shifted(p + 1) * before + pair(p) * after
                else:
                    tile = pair(p) * before + shifted(p) * after
            rd[pl.ds(64 * k, 64), pl.ds(128 * q, 128)] = tile

    starts = {NEXT: 18, PREV: 6, NEXT2: 24, PREV2: 0}

    def build_received(buffer, r):
        build(starts[buffer] + r, lambda p: rx[buffer, r, p])

    for r in range(6):
        build(REACH + r, lambda p, r=r: pk[r, p])

    scale = 0.6 / math.sqrt(24 * 64)
    spans = [(0, 18), (0, 24), (0, 30), (6, 30), (12, 30)]
    wide = lax.broadcasted_iota(jnp.int32, (1, 384), 1) // 64

    def partial(left, t, ranges):
        result = None
        for k0, k1 in ranges:
            if k1 > k0:
                product = jnp.dot(
                    left(64 * k0, 64 * k1),
                    rd[64 * k0 : 64 * k1, 384 * t : 384 * t + 384],
                    preferred_element_type=jnp.float32,
                )
                result = product if result is None else result + product
        return result

    mine = lambda a, b: rd[768:1152, a:b]

    def squares(late, zs, wait_early, wait_late):
        at_each_place(wait_early, zs)
        for buffer in starts:
            if buffer != late:
                for r in range(6):
                    build_received(buffer, r)
        first, last = starts[late], starts[late] + 6
        for t, (k0, k1) in enumerate(spans):
            early = [(k0, min(k1, first)), (max(k0, last), k1)]
            fin[:, 384 * t : 384 * t + 384] = partial(mine, t, early)
        for c in range(3):
            at_each_place(lambda p: wait_late(p, c), zs)
            for r in (2 * c, 2 * c + 1):
                build_received(late, r)
        for t, (k0, k1) in enumerate(spans):
            product = fin[:, 384 * t : 384 * t + 384]
            more = partial(mine, t, [(max(k0, first), min(k1, last))])
            if more is not None:
                product = product + more
            for r in range(6):
                w = wide + (6 * t - r)
                keep = (w >= 0) & (w <= 24) & (w != missing[REACH + r])
                part = product[64 * r : 64 * r + 64] * jnp.where(keep, scale, 0.0)
                sq_ref[64 * r : 64 * r + 64, 384 * t : 384 * t + 384] = part.astype(jnp.bfloat16)

    def early_work(late):
        def work(p):
            for t in p.transfers:
                if t[0] != OWN:
                    p.send(t)
            for c in range(3):
                for dst in starts:
                    if dst != late:
                        p.arrive_chunk(dst, c)

        return work

    def late_work(late):
        return lambda p, c: p.arrive_chunk(late, c)

    if relay:

        @pl.when(col < 2)
        def _():
            squares(PREV, (0, 1), early_work(PREV), late_work(PREV))

        @pl.when(col >= 2)
        def _():
            squares(NEXT, (2, 3), early_work(NEXT), late_work(NEXT))
    else:
        squares(PREV, (0,), early_work(PREV), late_work(PREV))

    for t, (k0, k1) in enumerate(spans):
        product = partial(lambda a, b: sq_ref[:, a:b], t, [(k0, k1)])
        square = sq_ref[:, 384 * t : 384 * t + 384].astype(jnp.float32)
        fin[:, 384 * t : 384 * t + 384] = 3.0 * square - (2.0 * scale) * product

    for r in range(6):
        m = missing[REACH + r]
        at = lambda c: fin[64 * r : 64 * r + 64, 64 * c : 64 * c + 64]
        for s in range(24):
            before = (s < m).astype(jnp.float32)
            out_ref[r, s] = (at(r + s) * before + at(r + s + 1) * (1.0 - before)).astype(jnp.bfloat16)

    def drain(p):
        for sent in p.started:
            p.copy(*sent).wait_send()

    at_each_place(drain)


def shards(n_rows, n_cols, values, columns):
    return pl.pallas_call(
        functools.partial(kernel, n_rows, n_cols),
        out_shape=jax.ShapeDtypeStruct(values.shape, jnp.bfloat16),
        in_specs=[pl.BlockSpec(memory_space=pl.ANY), pl.BlockSpec(memory_space=pltpu.VMEM)],
        out_specs=pl.BlockSpec(memory_space=pltpu.VMEM),
        scratch_shapes=[
            pltpu.VMEM(values.shape, jnp.bfloat16),
            pltpu.VMEM((6, 12, 64, 128), jnp.bfloat16),
            pltpu.VMEM((4, 6, 12, 64, 128), jnp.bfloat16),
            pltpu.VMEM((1920, 1920), jnp.bfloat16),
            pltpu.VMEM((384, 1920), jnp.bfloat16),
            pltpu.VMEM((384, 1920), jnp.float32),
            pltpu.SemaphoreType.DMA((3,)),
            pltpu.SemaphoreType.DMA((32,)),
            pltpu.SemaphoreType.DMA((4, 2, 3)),
        ],
        compiler_params=pltpu.CompilerParams(
            collective_id=0, has_side_effects=True, vmem_limit_bytes=60 * 1024 * 1024
        ),
    )(values, columns.T)


def solution(mesh):
    placed = (P(("row", "col"), None, None, None), P())
    return jax.shard_map(
        functools.partial(shards, mesh.shape["row"], mesh.shape["col"]),
        mesh=mesh,
        in_specs=placed,
        out_specs=P(("row", "col"), None, None, None),
        check_vma=False,
    )
```

time: 92.4 us -> 91.1 us (0.986)
  Pallas kernels: 88.3 us -> 86.7 us
    pallas_call x1, Pallas kernels: 88.3 us -> 86.7 us  [shards(): pl.pallas_call(functools.partial(kernel, n_rows, n_cols), out_shape=jax.S...]
    unnamed x4 -> x1, local copies, waits for them, and re-layouts: 3.9 us -> 3.87 us
where the time goes in v2:
time: 91.1 us; the launch traced here: 90.6 us
  Pallas kernels  86.7 us (95%)
  local copies, waits for them, and re-layouts  3.87 us (4%)
    pallas_call x1, Pallas kernels, shards(): pl.pallas_call(functools.partial(kernel, n_rows, n_cols), out_shape=jax.S...  86.7 us
    unnamed x1, local copies, waits for them, and re-layouts  3.87 us

profile of v2, /device:TPU:27, one launch (start us, length us, event | category | flops | bytes accessed | tf_op | source)
XLA Modules:
  0.0 90.6 jit_solution(1786803075895160360)
XLA Ops:
  0.0 86.7 %shard_map.28 = bf16[6,24,64,64]{3,2,1,0:T(8,128)(2,1)} custom-call(bf16[6,24,64,64]{3,2,1,0:T(8,128)(2,1)} %values_ref.1, s32[24,192]{1,0:T(8,128)} %bitcast.1), custom_call_target="tpu_custom_call" | custom-call | tf_op jit(solution)/shard_map/pallas_call | solution.py:326
  86.7 3.9 %copy.4 = bf16[6,24,64,64]{3,2,1,0:T(8,128)(2,1)} copy(bf16[6,24,64,64]{3,2,1,0:T(8,128)(2,1)} %shard_map.28) | data formatting | bytes 2359296

commit v3 on v2

--- a/solution.py
+++ b/solution.py
@@ -62,7 +62,7 @@
 
 
 def kernel(
-    n_rows, n_cols, values_ref, columns_ref, out_ref, vin, pk, rx, rd, sq_ref, fin, load_sem, send_sem, recv_sem
+    n_rows, n_cols, values_ref, columns_ref, out_ref, vin, pk, rx, rd, sq_ref, fin, band, load_sem, send_sem, recv_sem
 ):
     total = columns_ref.shape[1]
     row, col = lax.axis_index("row"), lax.axis_index("col")
@@ -234,8 +234,10 @@
         build(REACH + r, lambda p, r=r: pk[r, p])
 
     scale = 0.6 / math.sqrt(24 * 64)
-    spans = [(0, 18), (0, 24), (0, 30), (6, 30), (12, 30)]
-    wide = lax.broadcasted_iota(jnp.int32, (1, 384), 1) // 64
+    tiles = [(c, min(c + 4, 30)) for c in range(0, 30, 4)]
+    spans = [(max(0, c0 - REACH), min(30, c1 + REACH)) for c0, c1 in tiles]
+    wide = lax.broadcasted_iota(jnp.int32, (1, 256), 1) // 64
+    lanes = lambda t: slice(64 * tiles[t][0], 64 * tiles[t][1])
 
     def partial(left, t, ranges):
         result = None
@@ -243,7 +245,7 @@
             if k1 > k0:
                 product = jnp.dot(
                     left(64 * k0, 64 * k1),
-                    rd[64 * k0 : 64 * k1, 384 * t : 384 * t + 384],
+                    rd[64 * k0 : 64 * k1, lanes(t)],
                     preferred_element_type=jnp.float32,
                 )
                 result = product if result is None else result + product
@@ -260,21 +262,21 @@
         first, last = starts[late], starts[late] + 6
         for t, (k0, k1) in enumerate(spans):
             early = [(k0, min(k1, first)), (max(k0, last), k1)]
-            fin[:, 384 * t : 384 * t + 384] = partial(mine, t, early)
+            fin[:, lanes(t)] = partial(mine, t, early)
         for c in range(3):
             at_each_place(lambda p: wait_late(p, c), zs)
             for r in (2 * c, 2 * c + 1):
                 build_received(late, r)
         for t, (k0, k1) in enumerate(spans):
-            product = fin[:, 384 * t : 384 * t + 384]
+            product = fin[:, lanes(t)]
             more = partial(mine, t, [(max(k0, first), min(k1, last))])
             if more is not None:
                 product = product + more
             for r in range(6):
-                w = wide + (6 * t - r)
+                w = wide[:, : 64 * (tiles[t][1] - tiles[t][0])] + (tiles[t][0] - r)
                 keep = (w >= 0) & (w <= 24) & (w != missing[REACH + r])
                 part = product[64 * r : 64 * r + 64] * jnp.where(keep, scale, 0.0)
-                sq_ref[64 * r : 64 * r + 64, 384 * t : 384 * t + 384] = part.astype(jnp.bfloat16)
+                sq_ref[64 * r : 64 * r + 64, lanes(t)] = part.astype(jnp.bfloat16)
 
     def early_work(late):
         def work(p):
@@ -305,15 +307,17 @@
 
     for t, (k0, k1) in enumerate(spans):
         product = partial(lambda a, b: sq_ref[:, a:b], t, [(k0, k1)])
-        square = sq_ref[:, 384 * t : 384 * t + 384].astype(jnp.float32)
-        fin[:, 384 * t : 384 * t + 384] = 3.0 * square - (2.0 * scale) * product
+        square = sq_ref[:, lanes(t)].astype(jnp.float32)
+        band[:, lanes(t)] = (3.0 * square - (2.0 * scale) * product).astype(jnp.bfloat16)
 
     for r in range(6):
         m = missing[REACH + r]
-        at = lambda c: fin[64 * r : 64 * r + 64, 64 * c : 64 * c + 64]
+        at = lambda c: band[64 * r : 64 * r + 64, 64 * c : 64 * c + 64]
         for s in range(24):
-            before = (s < m).astype(jnp.float32)
-            out_ref[r, s] = (at(r + s) * before + at(r + s + 1) * (1.0 - before)).astype(jnp.bfloat16)
+            here = (lane[:, :64] * 0 + s) < m
+            before = here.astype(jnp.float32).astype(jnp.bfloat16)
+            after = 1.0 - here.astype(jnp.float32)
+            out_ref[r, s] = at(r + s) * before + at(r + s + 1) * after.astype(jnp.bfloat16)
 
     def drain(p):
         for sent in p.started:
@@ -326,7 +330,7 @@
     return pl.pallas_call(
         functools.partial(kernel, n_rows, n_cols),
         out_shape=jax.ShapeDtypeStruct(values.shape, jnp.bfloat16),
-        in_specs=[pl.BlockSpec(memory_space=pl.ANY), pl.BlockSpec(memory_space=pltpu.VMEM)],
+        in_specs=[pl.BlockSpec(memory_space=pltpu.HBM), pl.BlockSpec(memory_space=pltpu.VMEM)],
         out_specs=pl.BlockSpec(memory_space=pltpu.VMEM),
         scratch_shapes=[
             pltpu.VMEM(values.shape, jnp.bfloat16),
@@ -335,12 +339,13 @@
             pltpu.VMEM((1920, 1920), jnp.bfloat16),
             pltpu.VMEM((384, 1920), jnp.bfloat16),
             pltpu.VMEM((384, 1920), jnp.float32),
+            pltpu.VMEM((384, 1920), jnp.bfloat16),
             pltpu.SemaphoreType.DMA((3,)),
             pltpu.SemaphoreType.DMA((32,)),
             pltpu.SemaphoreType.DMA((4, 2, 3)),
         ],
         compiler_params=pltpu.CompilerParams(
-            collective_id=0, has_side_effects=True, vmem_limit_bytes=60 * 1024 * 1024
+            collective_id=0, has_side_effects=True, vmem_limit_bytes=48 * 1024 * 1024
         ),
     )(values, columns.T)
 

time: 91.1 us -> 88.6 us (0.973)
  Pallas kernels: 86.7 us -> 84.5 us
    pallas_call x1, Pallas kernels: 86.7 us -> 84.5 us  [shards(): pl.pallas_call(functools.partial(kernel, n_rows, n_cols), out_shape=jax.S...]
    unnamed x1 -> x5, local copies, waits for them, and re-layouts: 3.87 us -> 3.81 us
where the time goes in v3:
time: 88.6 us; the launch traced here: 88.4 us
  Pallas kernels  84.5 us (95%)
  local copies, waits for them, and re-layouts  3.81 us (4%)
    pallas_call x1, Pallas kernels, shards(): pl.pallas_call(functools.partial(kernel, n_rows, n_cols), out_shape=jax.S...  84.5 us
    unnamed x5, local copies, waits for them, and re-layouts  3.81 us

profile of v3, /device:TPU:27, one launch (start us, length us, event | category | flops | bytes accessed | tf_op | source)
XLA Modules:
  0.0 88.4 jit_solution(9956973708431604112)
XLA Ops:
  0.0 0.0 copy-start
  0.0 1.7 %copy-done = bf16[6,24,64,64]{3,2,1,0:T(8,128)(2,1)S(1)} copy-done((bf16[6,24,64,64]{3,2,1,0:T(8,128)(2,1)S(1)}, bf16[6,24,64,64]{3,2,1,0:T(8,128)(2,1)}, u32[]{:S(2)}) %copy-start) | copy-done | bytes 1179672
  1.7 0.0 copy-start.1
  1.7 0.7 copy-done.1
  2.4 84.5 %shard_map.28 = bf16[6,24,64,64]{3,2,1,0:T(8,128)(2,1)S(1)} custom-call(bf16[6,24,64,64]{3,2,1,0:T(8,128)(2,1)S(1)} %copy-done, s32[24,192]{1,0:T(8,128)S(1)} %bitcast.1), custom_call_target="tpu_custom_call" | custom-call | tf_op jit(solution)/shard_map/pallas_call | solution.py:330
  87.0 1.4 %copy.4 = bf16[6,24,64,64]{3,2,1,0:T(8,128)(2,1)} copy(bf16[6,24,64,64]{3,2,1,0:T(8,128)(2,1)S(1)} %shard_map.28) | data formatting | bytes 2359296
Async XLA Ops:
  0.0 1.7 %copy-start = (bf16[6,24,64,64]{3,2,1,0:T(8,128)(2,1)S(1)}, bf16[6,24,64,64]{3,2,1,0:T(8,128)(2,1)}, u32[]{:S(2)}) copy-start(bf16[6,24,64,64]{3,2,1,0:T(8,128)(2,1)} %values_ref.1) | copy-start | bytes 3538948
  1.7 0.7 copy-start.1
